TPU v7x, 512 devices: a whole 4x8x8 slice. The times are simulated.
512 devices in a mesh: sec: 8 (over y), rad: 16 (over z, x_hi), ax: 4 (over x_lo, core).
Axes of the slice: x: 4 (x_hi: 2, x_lo: 2; x = x_hi * 2 + x_lo), y: 8, z: 8, core: 2. Of those that a mesh axis runs over, the one named last changes fastest.
Arguments:
- state: float32 [5, 8, 1024, 2048], P(None, 'ax', 'rad', 'sec'), may hold values from -1.6 to 4, as said below
- coarsen: int32 [16], replicated, may hold values from 1 to 16, as said below
Outputs:
- tendency: float32 [5, 8, 1024, 2048], P(None, 'ax', 'rad', 'sec')
Inputs may be any that keep to these rules, and one draw needn't show every extreme that they name: `coarsen`: each entry is a power of two; cycle 0 takes 16 and cycle 16 - 1 takes 1. state[0] (density) lies in 0.6 to 1.4, the momenta in -1.6 to 1.6, state[4] (energy) in 2.5 to 4.0.
All inputs are finite; a program needn't handle non-finite values.
Results may differ from a plain program's by a relative error of at most 0.0003.
Values sent between devices are 32-bit elements; how exact they have to be, the bound alone decides.
A program may use at most 64 MiB of HBM per device.

v0:
```python
import math
import jax
import jax.numpy as jnp
from jax import lax
from jax.sharding import PartitionSpec as P

R_NEAR = 16
GAMMA = 1.4
KAPPA = 1.44


def padded_2(value, sides, width):
    for axis, dim in sides:
        size, length = (lax.axis_size(axis), value.shape[dim])
        up = [(i, (i + 1) % size) for i in range(size)]
        down = [(j, i) for i, j in up]
        last = lax.slice_in_dim(value, length - width, length, axis=dim)
        first = lax.slice_in_dim(value, 0, width, axis=dim)
        before = lax.ppermute(last, axis, up)
        after = lax.ppermute(first, axis, down)
        value = jnp.concatenate([before, value, after], axis=dim)
    return value


def spread(value, axis, root):
    mine = lax.axis_index(axis) == root
    return lax.psum(jnp.where(mine, value, jnp.zeros_like(value)), axis)


def body(state, coarsen):
    fields, planes, cycles_dev, cells_dev = state.shape
    sec_count = lax.axis_size("sec")
    rad_count = lax.axis_size("rad")
    ax_count = lax.axis_size("ax")
    sec_index = lax.axis_index("sec")
    rad_index = lax.axis_index("rad")
    ax_index = lax.axis_index("ax")
    total_cells = cells_dev * sec_count
    dtheta = 2.0 * math.pi / total_cells
    padded = padded_2(state, (("sec", 3), ("rad", 2), ("ax", 1)), 1)
    plane_pos = ax_index * planes + jnp.arange(-1, planes + 1, dtype=jnp.int32)
    cycle_pos = rad_index * cycles_dev + jnp.arange(-1, cycles_dev + 1, dtype=jnp.int32)
    inside_ax = ((plane_pos >= 0) & (plane_pos < planes * ax_count)).astype(jnp.float32)
    inside_rad = ((cycle_pos >= 0) & (cycle_pos < cycles_dev * rad_count)).astype(jnp.float32)
    ghost_plane = jnp.arange(planes + 2) % (planes + 1) == 0
    ghost_cycle = jnp.arange(cycles_dev + 2) % (cycles_dev + 1) == 0
    ghost_cell = jnp.arange(cells_dev + 2) % (cells_dev + 1) == 0
    ghosts = (
        ghost_plane.astype(jnp.int32)[:, None, None]
        + ghost_cycle.astype(jnp.int32)[None, :, None]
        + ghost_cell.astype(jnp.int32)[None, None, :]
    )
    corner = ghosts >= 2
    density = jnp.where(corner, 1.0, padded[0])
    mom_ax = padded[1]
    mom_rad = padded[2]
    mom_az = padded[3]
    energy = padded[4]
    vel_ax = mom_ax / density
    vel_rad = mom_rad / density
    vel_az = mom_az / density
    pressure = (GAMMA - 1.0) * (
        energy - 0.5 * (mom_ax * vel_ax + mom_rad * vel_rad + mom_az * vel_az)
    )
    radius_pad = cycle_pos.astype(jnp.float32) + 0.5
    flux_ax = jnp.stack(
        [
            mom_ax,
            mom_ax * vel_ax + pressure,
            mom_rad * vel_ax,
            mom_az * vel_ax,
            (energy + pressure) * vel_ax,
        ]
    )
    flux_ax = flux_ax * inside_ax[None, :, None, None]
    flux_rad = jnp.stack(
        [
            mom_rad,
            mom_ax * vel_rad,
            mom_rad * vel_rad + pressure,
            mom_az * vel_rad,
            (energy + pressure) * vel_rad,
        ]
    )
    flux_rad = flux_rad * (radius_pad * inside_rad)[None, None, :, None]
    flux_az = jnp.stack(
        [
            mom_az,
            mom_ax * vel_az,
            mom_rad * vel_az,
            mom_az * vel_az + pressure,
            (energy + pressure) * vel_az,
        ]
    )
    radius = radius_pad[1:-1][:, None]
    tendency = -(flux_ax[:, 2:, 1:-1, 1:-1] - flux_ax[:, :-2, 1:-1, 1:-1]) * 0.5
    tendency = (
        tendency - (flux_rad[:, 1:-1, 2:, 1:-1] - flux_rad[:, 1:-1, :-2, 1:-1]) * 0.5 / radius
    )
    tendency = tendency - (flux_az[:, 1:-1, 1:-1, 2:] - flux_az[:, 1:-1, 1:-1, :-2]) * 0.5 / (
        radius * dtheta
    )
    inner_press = pressure[1:-1, 1:-1, 1:-1]
    inner_mom_az = mom_az[1:-1, 1:-1, 1:-1]
    inner_mom_rad = mom_rad[1:-1, 1:-1, 1:-1]
    inner_vel_az = vel_az[1:-1, 1:-1, 1:-1]
    zero_part = jnp.zeros_like(inner_press)
    source = jnp.stack(
        [
            zero_part,
            zero_part,
            (inner_press + inner_mom_az * inner_vel_az) / radius,
            -(inner_mom_rad * inner_vel_az) / radius,
            zero_part,
        ]
    )
    tendency = tendency + source
    own_pos = sec_index * cells_dev + jnp.arange(cells_dev, dtype=jnp.int32)

    def kernel(cycle_factor, cycle_blocks, log_ratio, scale_const, columns):
        rows_coarse = own_pos // cycle_factor
        columns_coarse = columns // cycle_factor
        distance = ((rows_coarse[:, None] - columns_coarse[None, :]) % cycle_blocks).astype(
            jnp.float32
        )
        blocks_f = cycle_blocks.astype(jnp.float32)
        return (jnp.exp(distance * log_ratio) + jnp.exp((blocks_f - distance) * log_ratio)) / (
            scale_const * cycle_factor.astype(jnp.float32)
        )

    near_axis = tendency[:, :, :R_NEAR, :]
    cycle_lines = jnp.transpose(near_axis, (2, 0, 1, 3)).reshape(R_NEAR, fields * planes, cells_dev)
    shared = spread(cycle_lines, "rad", 0)
    per_device = R_NEAR // rad_count
    my_cycles = lax.dynamic_slice_in_dim(shared, rad_index * per_device, per_device, 0)
    selector = (rad_index * per_device + jnp.arange(per_device, dtype=jnp.int32))[
        :, None
    ] == jnp.arange(coarsen.shape[0], dtype=jnp.int32)[None, :]
    factor = jnp.sum(jnp.where(selector, coarsen[None, :], 0), axis=1)
    blocks = total_cells // factor
    factor_f = factor.astype(jnp.float32)
    stiffness = KAPPA / (factor_f * dtheta) ** 2
    inverse_half = 0.5 / stiffness
    one_minus = jnp.sqrt(inverse_half * (2.0 + inverse_half)) - inverse_half
    log_ratio = jnp.log1p(-one_minus)
    scale_const = (
        stiffness
        * one_minus
        * (2.0 - one_minus)
        / (1.0 - one_minus)
        * -jnp.expm1(blocks.astype(jnp.float32) * log_ratio)
    )
    portion = lax.all_gather(my_cycles, "sec", axis=2, tiled=True)
    columns = jnp.arange(portion.shape[2], dtype=jnp.int32)

    def per_cycle(cycle_item):
        lines_one, cycle_factor, cycle_blocks, cycle_log, cycle_scale = cycle_item
        table = kernel(cycle_factor, cycle_blocks, cycle_log, cycle_scale, columns)
        return jnp.einsum("lq,pq->lp", lines_one, table, precision=lax.Precision.HIGHEST)

    smoothed = lax.map(per_cycle, (portion, factor, blocks, log_ratio, scale_const))
    result = lax.all_gather(smoothed, "rad", axis=0, tiled=True)
    restored = jnp.transpose(result.reshape(R_NEAR, fields, planes, cells_dev), (1, 2, 0, 3))
    near_new = jnp.where(rad_index == 0, restored, near_axis)
    return jnp.concatenate([near_new, tendency[:, :, R_NEAR:, :]], axis=2)


def solution(mesh):
    return jax.shard_map(
        body,
        mesh=mesh,
        in_specs=(P(None, "ax", "rad", "sec"), P()),
        out_specs=P(None, "ax", "rad", "sec"),
        check_vma=False,
    )
```

profile of v0, /device:TPU:6, one launch (start us, length us, event | category | flops | bytes accessed | tf_op | source)
XLA Modules:
  0.0 309.1 jit_solution(6789559779002969412)
XLA Ops:
  6.5 0.0 copy-start
  6.5 0.0 all-reduce.2.cloned.1.call-start
  6.5 1.3 fusion.47
  7.8 3.5 %collective-permute-start = (f32[5,2,64,1]{3,2,1,0:T(8,128)S(1)}, f32[5,2,64,1]{3,2,1,0:T(8,128)S(1)}, u32[]{:S(2)}, u32[]{:S(2)}) collective-permute-start(f32[5,2,64,1]{3,2,1,0:T(8,128)S(1)} %get-tuple-element.59), channel_id=1, source_target_pairs={{0,64},{64,128},{128,192},{192,256},{256,320},{320,384},{384,448},... | collective-permute-start | bytes 7688 | tf_op jit(solution)/shard_map/ppermute | solution.py:19
  11.3 3.8 %collective-permute-start.1 = (f32[5,2,64,1]{3,2,1,0:T(8,128)S(1)}, f32[5,2,64,1]{3,2,1,0:T(8,128)S(1)}, u32[]{:S(2)}, u32[]{:S(2)}) collective-permute-start(f32[5,2,64,1]{3,2,1,0:T(8,128)S(1)} %get-tuple-element.60), channel_id=1, source_target_pairs={{64,0},{128,64},{192,128},{256,192},{320,256},{384,320},{448,384},... | collective-permute-start | bytes 7688 | tf_op jit(solution)/shard_map/ppermute | solution.py:20
  15.2 0.1 broadcast_multiply_fusion.2
  15.2 1.4 fusion.44
  16.6 4.3 %collective-permute-done = f32[5,2,64,1]{3,2,1,0:T(8,128)S(1)} collective-permute-done((f32[5,2,64,1]{3,2,1,0:T(8,128)S(1)}, f32[5,2,64,1]{3,2,1,0:T(8,128)S(1)}, u32[]{:S(2)}, u32[]{:S(2)}) %collective-permute-start) | collective-permute-done | bytes 2592 | tf_op jit(solution)/shard_map/ppermute | solution.py:19
  20.9 1.5 collective-permute-done.1
  22.4 1.1 pad_maximum_fusion.5
  23.5 5.1 %collective-permute-start.2 = (f32[5,2,1,258]{3,2,1,0:T(1,128)S(1)}, f32[5,2,1,258]{3,2,1,0:T(1,128)S(1)}, u32[]{:S(2)}, u32[]{:S(2)}) collective-permute-start(f32[5,2,1,258]{3,2,1,0:T(1,128)S(1)} %get-tuple-element.53), channel_id=1, source_target_pairs={{0,4},{4,8},{8,12},{12,16},{16,20},{20,24},{24,28},{28,32},{32,36}... | collective-permute-start | bytes 30968 | tf_op jit(solution)/shard_map/ppermute | solution.py:19
  28.6 2.2 collective-permute-start.3
  30.9 0.0 collective-permute-done.2
  30.9 5.8 %collective-permute-done.3 = f32[5,2,1,258]{3,2,1,0:T(1,128)S(1)} collective-permute-done((f32[5,2,1,258]{3,2,1,0:T(1,128)S(1)}, f32[5,2,1,258]{3,2,1,0:T(1,128)S(1)}, u32[]{:S(2)}, u32[]{:S(2)}) %collective-permute-start.3) | collective-permute-done | bytes 10352 | tf_op jit(solution)/shard_map/ppermute | solution.py:20
  36.6 0.0 copy-done
  36.6 0.5 pad_maximum_fusion.1
  37.1 0.1 fusion.46
  37.2 0.5 copy.5
  37.7 1.9 collective-permute-start.4
  39.6 0.5 copy.6
  40.2 3.6 %collective-permute-start.5 = (f32[5,1,66,258]{3,1,2,0:T(1,128)S(1)}, f32[5,1,66,258]{3,1,2,0:T(1,128)S(1)}, u32[]{:S(2)}, u32[]{:S(2)}) collective-permute-start(f32[5,1,66,258]{3,1,2,0:T(1,128)S(1)} %copy.6), channel_id=1, source_target_pairs={{1,0},{2,1},{3,2},{0,3},{5,4},{6,5},{7,6},{4,7},{9,8},{10,9},{11,1... | collective-permute-start | bytes 1021688 | tf_op jit(solution)/shard_map/ppermute | solution.py:20
  43.9 0.1 pad.5.clone
  44.7 0.1 broadcast_add_fusion
  44.7 6.0 %collective-permute-done.4 = f32[5,1,66,258]{3,1,2,0:T(1,128)S(1)} collective-permute-done((f32[5,1,66,258]{3,1,2,0:T(1,128)S(1)}, f32[5,1,66,258]{3,1,2,0:T(1,128)S(1)}, u32[]{:S(2)}, u32[]{:S(2)}) %collective-permute-start.4) | collective-permute-done | bytes 340592 | tf_op jit(solution)/shard_map/ppermute | solution.py:19
  50.8 0.1 collective-permute-done.5
  51.0 0.5 pad_maximum_fusion
  51.5 0.2 slice_bitcast_fusion.3
  51.7 0.2 fusion.28
  51.9 0.3 add_dynamic-update-slice_fusion.2
  52.2 0.1 multiply_dynamic-update-slice_fusion.8
  52.2 0.1 multiply_dynamic-update-slice_fusion.7
  52.4 0.1 multiply_dynamic-update-slice_fusion.1
  52.4 0.1 add_dynamic-update-slice_fusion
  52.5 0.2 multiply_dynamic-update-slice_fusion.6
  52.7 0.1 multiply_dynamic-update-slice_fusion.4
  52.8 0.1 multiply_dynamic-update-slice_fusion.3
  52.9 0.4 broadcast_multiply_fusion
  53.3 0.3 fusion.32
  53.6 1.1 fusion.19
  54.7 0.7 slice_select_fusion.1
  55.4 0.0 all-reduce.2.cloned.1.call-update
  55.4 0.8 and_select_fusion
  58.5 0.8 add_select_fusion.1
  59.4 161.4 %all-reduce.2.cloned.1.call-done = f32[16,10,256]{2,0,1:T(8,128)} async-done(((f32[16,10,256]{2,0,1:T(8,128)}), f32[16,10,256]{2,0,1:T(8,128)}) %all-reduce.2.cloned.1.call-update) | async-done | bytes 163856 | tf_op jit(solution)/shard_map/psum | solution.py:27
  220.8 0.9 constant_dynamic-slice_fusion
  221.7 16.7 %all_gather.6 = f32[1,10,2048]{2,0,1:T(1,128)S(1)} all-gather(f32[1,10,256]{2,0,1:T(1,128)S(1)} %constant_dynamic-slice_fusion), channel_id=1, replica_groups=mesh['sec'=8,'rad'=16,'ax'=4] {'sec'}, dimensions={2}, use_global_device_ids=true | all-gather | bytes 92160 | tf_op jit(solution)/shard_map/all_gather | solution.py:153
  238.4 22.6 %fusion.7 = f32[1,10,256]{2,1,0:T(8,128)S(1)} fusion(f32[]{:T(128)S(6)} %mul.233, f32[]{:T(128)S(6)} %convert_element_type.66, f32[]{:T(128)} %bitcast.13, s32[]{:T(128)S(6)} %select_n.132, s32[2048]{0:T(1024)S(1)} %add_select_fusion.1, s32[256]{0:T(256)S(1)} %and_select_fusion, pred[]{:T(512)S(6)} %lt.63, f32[1,10,2048]{2,0,1:T(1,128)S(1)} %all_gather.6), kind=kOutput, calls=%fused_computation.10 | convolution fusion | flops 70254592 | bytes 101393 | tf_op jit(solution)/shard_map/while/body/eval_jaxpr/lq,pq->lp/dot_general | solution.py:159
  261.0 40.3 %all-gather.1 = f32[16,10,256]{2,1,0:T(8,128)S(1)} all-gather(f32[1,10,256]{2,1,0:T(8,128)S(1)} %fusion.7), channel_id=2, replica_groups=mesh['sec'=8,'rad'=16,'ax'=4] {'rad'}, dimensions={0}, use_global_device_ids=true | all-gather | bytes 174080 | tf_op jit(solution)/shard_map/all_gather | solution.py:162
  301.2 0.1 copy.9
  301.4 0.9 pad_maximum_fusion.2
  (12 shorter events, 0.2 us)
Async XLA Ops:
  6.5 30.1 %copy-start = (f32[5,2,64,256]{3,2,1,0:T(8,128)S(1)}, f32[5,2,64,256]{3,2,1,0:T(8,128)}, u32[]{:S(2)}) copy-start(f32[5,2,64,256]{3,2,1,0:T(8,128)} %param.2) | copy-start | bytes 1966084
  6.5 214.2 %all-reduce.2.cloned.1.call-start = ((), (), s32[]{:S(2)}) async-start(), calls=%async_computation | async-start | bytes 327680 | tf_op jit(solution)/shard_map/psum | solution.py:27
  7.8 13.1 %collective-permute-start = (f32[5,2,64,1]{3,2,1,0:T(8,128)S(1)}, f32[5,2,64,1]{3,2,1,0:T(8,128)S(1)}, u32[]{:S(2)}, u32[]{:S(2)}) collective-permute-start(f32[5,2,64,1]{3,2,1,0:T(8,128)S(1)} %get-tuple-element.59), channel_id=1, source_target_pairs={{0,64},{64,128},{128,192},{192,256},{256,320},{320,384},{384,448},... | collective-permute-start | bytes 7688 | tf_op jit(solution)/shard_map/ppermute | solution.py:19
  11.3 11.1 %collective-permute-start.1 = (f32[5,2,64,1]{3,2,1,0:T(8,128)S(1)}, f32[5,2,64,1]{3,2,1,0:T(8,128)S(1)}, u32[]{:S(2)}, u32[]{:S(2)}) collective-permute-start(f32[5,2,64,1]{3,2,1,0:T(8,128)S(1)} %get-tuple-element.60), channel_id=1, source_target_pairs={{64,0},{128,64},{192,128},{256,192},{320,256},{384,320},{448,384},... | collective-permute-start | bytes 7688 | tf_op jit(solution)/shard_map/ppermute | solution.py:20
  23.5 7.4 %collective-permute-start.2 = (f32[5,2,1,258]{3,2,1,0:T(1,128)S(1)}, f32[5,2,1,258]{3,2,1,0:T(1,128)S(1)}, u32[]{:S(2)}, u32[]{:S(2)}) collective-permute-start(f32[5,2,1,258]{3,2,1,0:T(1,128)S(1)} %get-tuple-element.53), channel_id=1, source_target_pairs={{0,4},{4,8},{8,12},{12,16},{16,20},{20,24},{24,28},{28,32},{32,36}... | collective-permute-start | bytes 30968 | tf_op jit(solution)/shard_map/ppermute | solution.py:19
  28.6 8.0 %collective-permute-start.3 = (f32[5,2,1,258]{3,2,1,0:T(1,128)S(1)}, f32[5,2,1,258]{3,2,1,0:T(1,128)S(1)}, u32[]{:S(2)}, u32[]{:S(2)}) collective-permute-start(f32[5,2,1,258]{3,2,1,0:T(1,128)S(1)} %get-tuple-element.54), channel_id=1, source_target_pairs={{4,0},{8,4},{12,8},{16,12},{20,16},{24,20},{28,24},{32,28},{36,32}... | collective-permute-start | bytes 30968 | tf_op jit(solution)/shard_map/ppermute | solution.py:20
  37.7 13.0 %collective-permute-start.4 = (f32[5,1,66,258]{3,1,2,0:T(1,128)S(1)}, f32[5,1,66,258]{3,1,2,0:T(1,128)S(1)}, u32[]{:S(2)}, u32[]{:S(2)}) collective-permute-start(f32[5,1,66,258]{3,1,2,0:T(1,128)S(1)} %copy.5), channel_id=1, source_target_pairs={{0,1},{1,2},{2,3},{3,0},{4,5},{5,6},{6,7},{7,4},{8,9},{9,10},{10,1... | collective-permute-start | bytes 1021688 | tf_op jit(solution)/shard_map/ppermute | solution.py:19
  40.2 10.7 %collective-permute-start.5 = (f32[5,1,66,258]{3,1,2,0:T(1,128)S(1)}, f32[5,1,66,258]{3,1,2,0:T(1,128)S(1)}, u32[]{:S(2)}, u32[]{:S(2)}) collective-permute-start(f32[5,1,66,258]{3,1,2,0:T(1,128)S(1)} %copy.6), channel_id=1, source_target_pairs={{1,0},{2,1},{3,2},{0,3},{5,4},{6,5},{7,6},{4,7},{9,8},{10,9},{11,1... | collective-permute-start | bytes 1021688 | tf_op jit(solution)/shard_map/ppermute | solution.py:20
Sparse Core Ops, SparseCore 0:
  55.5 165.2 all-reduce.1
where the time goes:
time: 310 us; the launch traced here: 309 us
  waiting for transfers between devices  179 us (58%)
  blocking collectives  57 us (18%)
  matrix products  22.6 us (7%)
  starting transfers between devices  20.2 us (7%)
  between operations  16.7 us (5%)
  other arithmetic  9.79 us (3%)
  local copies, waits for them, and re-layouts  3.82 us (1%)
    psum x1, waiting for transfers between devices, spread(): return lax.psum(jnp.where(mine, value, jnp.zeros_like(value)), axis)  161 us
    all_gather x1, blocking collectives, body(): result = lax.all_gather(smoothed, 'rad', axis=0, tiled=True)  40.3 us
    dot_general x1, matrix products, per_cycle(): jnp.einsum('lq,pq->lp', lines_one, table, precision=lax.Precision.HIGHEST)  22.6 us
    all_gather x1, blocking collectives, body(): portion = lax.all_gather(my_cycles, 'sec', axis=2, tiled=True)  16.7 us
    ppermute x3, starting transfers between devices, padded_2(): before = lax.ppermute(last, axis, up)  10.5 us
    ppermute x3, waiting for transfers between devices, padded_2(): before = lax.ppermute(last, axis, up)  10.3 us
    ppermute x3, starting transfers between devices, padded_2(): after = lax.ppermute(first, axis, down)  9.68 us
    ppermute x3, waiting for transfers between devices, padded_2(): after = lax.ppermute(first, axis, down)  7.38 us
  transfers between devices with their start and end apart: 7, of which 6 were waited for; matrix products, arithmetic and copies ran while one was open for 1% of the time, Pallas kernels for 0%

commit v1 on v0

--- a/solution.py
+++ b/solution.py
@@ -7,6 +7,24 @@
 R_NEAR = 16
 GAMMA = 1.4
 KAPPA = 1.44
+
+
+def in_order(parts, dim):
+    parts = jnp.moveaxis(parts, 0, dim)
+    shape = parts.shape
+    return parts.reshape(*shape[:dim], shape[dim] * shape[dim + 1], *shape[dim + 2 :])
+
+
+def collected_by_bits(x, axis):
+    size = lax.axis_size(axis)
+    pieces = x[None]
+    for level in range(size.bit_length() - 1):
+        bit = 1 << level
+        other = lax.ppermute(pieces, axis, [(i, i ^ bit) for i in range(size)])
+        both = jnp.stack([pieces, other])
+        upper = lax.axis_index(axis) >> level & 1
+        pieces = jnp.where(upper == 0, both, both[::-1]).reshape(-1, *x.shape)
+    return pieces
 
 
 def padded_2(value, sides, width):
@@ -150,7 +168,7 @@
         / (1.0 - one_minus)
         * -jnp.expm1(blocks.astype(jnp.float32) * log_ratio)
     )
-    portion = lax.all_gather(my_cycles, "sec", axis=2, tiled=True)
+    portion = in_order(collected_by_bits(my_cycles, "sec"), 2)
     columns = jnp.arange(portion.shape[2], dtype=jnp.int32)
 
     def per_cycle(cycle_item):

time: 310 us -> 317 us (1.023)
  blocking collectives: 57 us -> 40.3 us
  starting transfers between devices: 20.2 us -> 35.5 us
  waiting for transfers between devices: 179 us -> 187 us
    all_gather x1 -> x0, blocking collectives: 16.7 us -> none  [body(): portion = lax.all_gather(my_cycles, 'sec', axis=2, tiled=True)]
    ppermute x0 -> x3, starting transfers between devices: none -> 15.3 us  [collected_by_bits(): other = lax.ppermute(pieces, axis, [(i, i ^ bit) for i in range(size)])]
    psum x1, waiting for transfers between devices: 161 us -> 165 us  [spread(): return lax.psum(jnp.where(mine, value, jnp.zeros_like(value)), axis)]
  transfers between devices with their start and end apart: 7 -> 10, of which waited for: 6 -> 8; matrix products, arithmetic and copies ran while one was open for 1% -> 1% of each run, Pallas kernels for 0% -> 0%
where the time goes in v1:
time: 317 us; the launch traced here: 316 us
  waiting for transfers between devices  187 us (59%)
  blocking collectives  40.3 us (13%)
  starting transfers between devices  35.5 us (11%)
  matrix products  22.6 us (7%)
  between operations  16.6 us (5%)
  other arithmetic  9.25 us (3%)
  local copies, waits for them, and re-layouts  4.43 us (1%)
    psum x1, waiting for transfers between devices, spread(): return lax.psum(jnp.where(mine, value, jnp.zeros_like(value)), axis)  165 us
    all_gather x1, blocking collectives, body(): result = lax.all_gather(smoothed, 'rad', axis=0, tiled=True)  40.3 us
    dot_general x1, matrix products, per_cycle(): jnp.einsum('lq,pq->lp', lines_one, table, precision=lax.Precision.HIGHEST)  22.6 us
    ppermute x3, starting transfers between devices, collected_by_bits(): other = lax.ppermute(pieces, axis, [(i, i ^ bit) for i in range(size)])  15.3 us
    ppermute x3, waiting for transfers between devices, padded_2(): before = lax.ppermute(last, axis, up)  12.4 us
    ppermute x3, starting transfers between devices, padded_2(): before = lax.ppermute(last, axis, up)  10.5 us
    ppermute x3, starting transfers between devices, padded_2(): after = lax.ppermute(first, axis, down)  9.68 us
    ppermute x3, waiting for transfers between devices, padded_2(): after = lax.ppermute(first, axis, down)  7.38 us
  transfers between devices with their start and end apart: 10, of which 8 were waited for; matrix products, arithmetic and copies ran while one was open for 1% of the time, Pallas kernels for 0%

profile of v1, /device:TPU:6, one launch (start us, length us, event | category | flops | bytes accessed | tf_op | source)
XLA Modules:
  0.0 316.2 jit_solution(1509740572476462167)
XLA Ops:
  6.5 0.0 copy-start
  6.5 0.0 all-reduce.2.cloned.1.call-start
  6.5 1.3 fusion.47
  7.8 3.5 %collective-permute-start = (f32[5,2,64,1]{3,2,1,0:T(8,128)S(1)}, f32[5,2,64,1]{3,2,1,0:T(8,128)S(1)}, u32[]{:S(2)}, u32[]{:S(2)}) collective-permute-start(f32[5,2,64,1]{3,2,1,0:T(8,128)S(1)} %get-tuple-element.59), channel_id=1, source_target_pairs={{0,64},{64,128},{128,192},{192,256},{256,320},{320,384},{384,448},... | collective-permute-start | bytes 7688 | tf_op jit(solution)/shard_map/ppermute | solution.py:37
  11.3 3.8 %collective-permute-start.1 = (f32[5,2,64,1]{3,2,1,0:T(8,128)S(1)}, f32[5,2,64,1]{3,2,1,0:T(8,128)S(1)}, u32[]{:S(2)}, u32[]{:S(2)}) collective-permute-start(f32[5,2,64,1]{3,2,1,0:T(8,128)S(1)} %get-tuple-element.60), channel_id=1, source_target_pairs={{64,0},{128,64},{192,128},{256,192},{320,256},{384,320},{448,384},... | collective-permute-start | bytes 7688 | tf_op jit(solution)/shard_map/ppermute | solution.py:38
  15.2 0.1 broadcast_multiply_fusion.2
  15.3 5.6 %collective-permute-done = f32[5,2,64,1]{3,2,1,0:T(8,128)S(1)} collective-permute-done((f32[5,2,64,1]{3,2,1,0:T(8,128)S(1)}, f32[5,2,64,1]{3,2,1,0:T(8,128)S(1)}, u32[]{:S(2)}, u32[]{:S(2)}) %collective-permute-start) | collective-permute-done | bytes 2592 | tf_op jit(solution)/shard_map/ppermute | solution.py:37
  20.9 1.5 collective-permute-done.1
  22.4 1.1 pad_maximum_fusion.8
  23.5 5.1 %collective-permute-start.2 = (f32[5,2,1,258]{3,2,1,0:T(1,128)S(1)}, f32[5,2,1,258]{3,2,1,0:T(1,128)S(1)}, u32[]{:S(2)}, u32[]{:S(2)}) collective-permute-start(f32[5,2,1,258]{3,2,1,0:T(1,128)S(1)} %get-tuple-element.53), channel_id=1, source_target_pairs={{0,4},{4,8},{8,12},{12,16},{16,20},{20,24},{24,28},{28,32},{32,36}... | collective-permute-start | bytes 30968 | tf_op jit(solution)/shard_map/ppermute | solution.py:37
  28.6 2.2 collective-permute-start.3
  30.9 0.0 collective-permute-done.2
  30.9 5.8 %collective-permute-done.3 = f32[5,2,1,258]{3,2,1,0:T(1,128)S(1)} collective-permute-done((f32[5,2,1,258]{3,2,1,0:T(1,128)S(1)}, f32[5,2,1,258]{3,2,1,0:T(1,128)S(1)}, u32[]{:S(2)}, u32[]{:S(2)}) %collective-permute-start.3) | collective-permute-done | bytes 10352 | tf_op jit(solution)/shard_map/ppermute | solution.py:38
  36.6 0.0 copy-done
  36.6 0.5 pad_maximum_fusion.1
  37.1 0.1 fusion.46
  37.2 0.5 copy.8
  37.7 1.9 collective-permute-start.4
  39.6 0.5 copy.9
  40.2 3.6 %collective-permute-start.5 = (f32[5,1,66,258]{3,1,2,0:T(1,128)S(1)}, f32[5,1,66,258]{3,1,2,0:T(1,128)S(1)}, u32[]{:S(2)}, u32[]{:S(2)}) collective-permute-start(f32[5,1,66,258]{3,1,2,0:T(1,128)S(1)} %copy.9), channel_id=1, source_target_pairs={{1,0},{2,1},{3,2},{0,3},{5,4},{6,5},{7,6},{4,7},{9,8},{10,9},{11,1... | collective-permute-start | bytes 1021688 | tf_op jit(solution)/shard_map/ppermute | solution.py:38
  43.9 0.1 pad.11.clone
  43.9 0.1 broadcast_add_fusion
  44.0 6.7 %collective-permute-done.4 = f32[5,1,66,258]{3,1,2,0:T(1,128)S(1)} collective-permute-done((f32[5,1,66,258]{3,1,2,0:T(1,128)S(1)}, f32[5,1,66,258]{3,1,2,0:T(1,128)S(1)}, u32[]{:S(2)}, u32[]{:S(2)}) %collective-permute-start.4) | collective-permute-done | bytes 340592 | tf_op jit(solution)/shard_map/ppermute | solution.py:37
  50.8 0.1 collective-permute-done.5
  51.0 0.5 pad_maximum_fusion
  51.4 0.2 slice_bitcast_fusion.3
  51.7 0.2 fusion.28
  51.9 0.3 add_dynamic-update-slice_fusion.2
  52.2 0.1 multiply_dynamic-update-slice_fusion.8
  52.2 0.1 multiply_dynamic-update-slice_fusion.7
  52.4 0.1 multiply_dynamic-update-slice_fusion.1
  52.4 0.1 add_dynamic-update-slice_fusion
  52.5 0.2 multiply_dynamic-update-slice_fusion.6
  52.7 0.1 multiply_dynamic-update-slice_fusion.4
  52.8 0.1 multiply_dynamic-update-slice_fusion.3
  52.8 0.4 broadcast_multiply_fusion
  53.3 0.3 fusion.32
  53.6 0.0 copy-start.1
  53.6 1.1 fusion.19
  54.7 0.7 slice_select_fusion.1
  55.4 0.0 all-reduce.2.cloned.1.call-update
  55.4 165.4 %all-reduce.2.cloned.1.call-done = f32[16,10,256]{2,0,1:T(8,128)} async-done(((f32[16,10,256]{2,0,1:T(8,128)}), f32[16,10,256]{2,0,1:T(8,128)}) %all-reduce.2.cloned.1.call-update) | async-done | bytes 163856 | tf_op jit(solution)/shard_map/psum | solution.py:45
  220.8 0.9 dynamic-slice_bitcast_fusion.1
  221.7 3.4 %collective-permute-start.6 = (f32[1,1,10,256]{3,1,2,0:T(1,128)S(1)}, f32[1,1,10,256]{3,1,2,0:T(1,128)S(1)}, u32[]{:S(2)}, u32[]{:S(2)}) collective-permute-start(f32[1,1,10,256]{3,1,2,0:T(1,128)S(1)} %get-tuple-element.62), channel_id=1, source_target_pairs={{0,64},{64,0},{128,192},{192,128},{256,320},{320,256},{384,448},{4... | collective-permute-start | bytes 30728 | tf_op jit(solution)/shard_map/ppermute | solution.py:23
  225.1 0.0 copy-done.1
  225.1 0.6 fusion.44
  226.4 0.9 collective-permute-done.6
  227.3 4.3 %collective-permute-start.7 = (f32[2,1,10,256]{3,1,2,0:T(1,128)S(1)}, f32[2,1,10,256]{3,1,2,0:T(1,128)S(1)}, u32[]{:S(2)}, u32[]{:S(2)}) collective-permute-start(f32[2,1,10,256]{3,1,2,0:T(1,128)S(1)} %get-tuple-element.64), channel_id=1, source_target_pairs={{0,128},{64,192},{128,0},{192,64},{256,384},{320,448},{384,256},{4... | collective-permute-start | bytes 61448 | tf_op jit(solution)/shard_map/ppermute | solution.py:23
  231.7 0.8 add_select_fusion.1
  232.4 1.5 collective-permute-done.7
  234.0 7.6 %collective-permute-start.8 = (f32[4,1,10,256]{3,1,2,0:T(1,128)S(1)}, f32[4,1,10,256]{3,1,2,0:T(1,128)S(1)}, u32[]{:S(2)}, u32[]{:S(2)}) collective-permute-start(f32[4,1,10,256]{3,1,2,0:T(1,128)S(1)} %bitcast.68), channel_id=1, source_target_pairs={{0,256},{64,320},{128,384},{192,448},{256,0},{320,64},{384,128},{4... | collective-permute-start | bytes 122888 | tf_op jit(solution)/shard_map/ppermute | solution.py:23
  241.6 0.8 and_select_fusion
  244.6 0.0 collective-permute-done.8
  244.6 0.1 pad_maximum_fusion.3
  244.7 0.5 rev.11
  245.2 0.1 broadcast_select_fusion.1
  245.3 0.1 copy.12
  245.4 22.6 %fusion.7 = f32[1,10,256]{2,1,0:T(8,128)S(1)} fusion(f32[10,2048]{1,0:T(8,128)S(1)} %bitcast.75, f32[]{:T(128)S(6)} %mul.233, f32[]{:T(128)S(6)} %convert_element_type.66, f32[]{:T(128)} %bitcast.24, s32[]{:T(128)S(6)} %select_n.162, s32[2048]{0:T(1024)S(1)} %add_select_fusion.1, s32[256]{0:T(256)S(1)} %and_select_fusion, pred[]{:T(512)S(6)} %lt.63), kind=kOutput, calls=%fused_computation.10 | convolution fusion | flops 70254592 | bytes 101393 | tf_op jit(solution)/shard_map/while/body/eval_jaxpr/lq,pq->lp/dot_general | solution.py:177
  268.0 40.3 %all-gather.1 = f32[16,10,256]{2,1,0:T(8,128)S(1)} all-gather(f32[1,10,256]{2,1,0:T(8,128)S(1)} %fusion.7), channel_id=2, replica_groups=mesh['sec'=8,'rad'=16,'ax'=4] {'rad'}, dimensions={0}, use_global_device_ids=true | all-gather | bytes 174080 | tf_op jit(solution)/shard_map/all_gather | solution.py:180
  308.3 0.1 copy.14
  308.4 0.9 pad_maximum_fusion.2
  (19 shorter events, 0.4 us)
Async XLA Ops:
  6.5 30.1 %copy-start = (f32[5,2,64,256]{3,2,1,0:T(8,128)S(1)}, f32[5,2,64,256]{3,2,1,0:T(8,128)}, u32[]{:S(2)}) copy-start(f32[5,2,64,256]{3,2,1,0:T(8,128)} %param.2) | copy-start | bytes 1966084
  6.5 214.3 %all-reduce.2.cloned.1.call-start = ((), (), s32[]{:S(2)}) async-start(), calls=%async_computation | async-start | bytes 327680 | tf_op jit(solution)/shard_map/psum | solution.py:45
  7.8 13.1 %collective-permute-start = (f32[5,2,64,1]{3,2,1,0:T(8,128)S(1)}, f32[5,2,64,1]{3,2,1,0:T(8,128)S(1)}, u32[]{:S(2)}, u32[]{:S(2)}) collective-permute-start(f32[5,2,64,1]{3,2,1,0:T(8,128)S(1)} %get-tuple-element.59), channel_id=1, source_target_pairs={{0,64},{64,128},{128,192},{192,256},{256,320},{320,384},{384,448},... | collective-permute-start | bytes 7688 | tf_op jit(solution)/shard_map/ppermute | solution.py:37
  11.3 11.1 %collective-permute-start.1 = (f32[5,2,64,1]{3,2,1,0:T(8,128)S(1)}, f32[5,2,64,1]{3,2,1,0:T(8,128)S(1)}, u32[]{:S(2)}, u32[]{:S(2)}) collective-permute-start(f32[5,2,64,1]{3,2,1,0:T(8,128)S(1)} %get-tuple-element.60), channel_id=1, source_target_pairs={{64,0},{128,64},{192,128},{256,192},{320,256},{384,320},{448,384},... | collective-permute-start | bytes 7688 | tf_op jit(solution)/shard_map/ppermute | solution.py:38
  23.5 7.4 %collective-permute-start.2 = (f32[5,2,1,258]{3,2,1,0:T(1,128)S(1)}, f32[5,2,1,258]{3,2,1,0:T(1,128)S(1)}, u32[]{:S(2)}, u32[]{:S(2)}) collective-permute-start(f32[5,2,1,258]{3,2,1,0:T(1,128)S(1)} %get-tuple-element.53), channel_id=1, source_target_pairs={{0,4},{4,8},{8,12},{12,16},{16,20},{20,24},{24,28},{28,32},{32,36}... | collective-permute-start | bytes 30968 | tf_op jit(solution)/shard_map/ppermute | solution.py:37
  28.6 8.0 %collective-permute-start.3 = (f32[5,2,1,258]{3,2,1,0:T(1,128)S(1)}, f32[5,2,1,258]{3,2,1,0:T(1,128)S(1)}, u32[]{:S(2)}, u32[]{:S(2)}) collective-permute-start(f32[5,2,1,258]{3,2,1,0:T(1,128)S(1)} %get-tuple-element.54), channel_id=1, source_target_pairs={{4,0},{8,4},{12,8},{16,12},{20,16},{24,20},{28,24},{32,28},{36,32}... | collective-permute-start | bytes 30968 | tf_op jit(solution)/shard_map/ppermute | solution.py:38
  37.7 13.0 %collective-permute-start.4 = (f32[5,1,66,258]{3,1,2,0:T(1,128)S(1)}, f32[5,1,66,258]{3,1,2,0:T(1,128)S(1)}, u32[]{:S(2)}, u32[]{:S(2)}) collective-permute-start(f32[5,1,66,258]{3,1,2,0:T(1,128)S(1)} %copy.8), channel_id=1, source_target_pairs={{0,1},{1,2},{2,3},{3,0},{4,5},{5,6},{6,7},{7,4},{8,9},{9,10},{10,1... | collective-permute-start | bytes 1021688 | tf_op jit(solution)/shard_map/ppermute | solution.py:37
  40.2 10.7 %collective-permute-start.5 = (f32[5,1,66,258]{3,1,2,0:T(1,128)S(1)}, f32[5,1,66,258]{3,1,2,0:T(1,128)S(1)}, u32[]{:S(2)}, u32[]{:S(2)}) collective-permute-start(f32[5,1,66,258]{3,1,2,0:T(1,128)S(1)} %copy.9), channel_id=1, source_target_pairs={{1,0},{2,1},{3,2},{0,3},{5,4},{6,5},{7,6},{4,7},{9,8},{10,9},{11,1... | collective-permute-start | bytes 1021688 | tf_op jit(solution)/shard_map/ppermute | solution.py:38
  53.6 171.5 %copy-start.1 = (s32[16]{0:T(128)S(1)}, s32[16]{0:T(128)}, u32[]{:S(2)}) copy-start(s32[16]{0:T(128)} %param.3) | copy-start | bytes 196
  221.7 5.6 %collective-permute-start.6 = (f32[1,1,10,256]{3,1,2,0:T(1,128)S(1)}, f32[1,1,10,256]{3,1,2,0:T(1,128)S(1)}, u32[]{:S(2)}, u32[]{:S(2)}) collective-permute-start(f32[1,1,10,256]{3,1,2,0:T(1,128)S(1)} %get-tuple-element.62), channel_id=1, source_target_pairs={{0,64},{64,0},{128,192},{192,128},{256,320},{320,256},{384,448},{4... | collective-permute-start | bytes 30728 | tf_op jit(solution)/shard_map/ppermute | solution.py:23
  227.3 6.6 %collective-permute-start.7 = (f32[2,1,10,256]{3,1,2,0:T(1,128)S(1)}, f32[2,1,10,256]{3,1,2,0:T(1,128)S(1)}, u32[]{:S(2)}, u32[]{:S(2)}) collective-permute-start(f32[2,1,10,256]{3,1,2,0:T(1,128)S(1)} %get-tuple-element.64), channel_id=1, source_target_pairs={{0,128},{64,192},{128,0},{192,64},{256,384},{320,448},{384,256},{4... | collective-permute-start | bytes 61448 | tf_op jit(solution)/shard_map/ppermute | solution.py:23
  234.0 10.6 %collective-permute-start.8 = (f32[4,1,10,256]{3,1,2,0:T(1,128)S(1)}, f32[4,1,10,256]{3,1,2,0:T(1,128)S(1)}, u32[]{:S(2)}, u32[]{:S(2)}) collective-permute-start(f32[4,1,10,256]{3,1,2,0:T(1,128)S(1)} %bitcast.68), channel_id=1, source_target_pairs={{0,256},{64,320},{128,384},{192,448},{256,0},{320,64},{384,128},{4... | collective-permute-start | bytes 122888 | tf_op jit(solution)/shard_map/ppermute | solution.py:23
Sparse Core Ops, SparseCore 0:
  55.5 165.2 all-reduce.1
